TPU v7x, 128 devices: a whole 4x4x4 slice. The times are simulated.
128 devices in a mesh: grp: 16 (over z, x_lo, core), col: 8 (over x_hi, y).
Axes of the slice: x: 4 (x_hi: 2, x_lo: 2; x = x_hi * 2 + x_lo), y: 4, z: 4, core: 2. Of those that a mesh axis runs over, the one named last changes fastest.
Arguments:
- constraint_rows: float32 [4096, 16384], P('grp', 'col'), may hold values from -0.125 to 0.125
- shift: float32 [16384], P('col'), may hold values from 0.3 to 1
- group_rows: int32 [16], replicated, may hold values from 1 to 256, 2048 in all
- panel_index: int32 [1], replicated, may hold values from 0 to 31
Outputs:
- panel_factor: float32 [16384, 512], P(('col', 'grp'))
Inputs may be any that keep to these rules, and one draw needn't show every extreme that they name: `group_rows`: the values sum to 2048 and the largest equals 256.
All inputs are finite; a program needn't handle non-finite values.
Results may differ from a plain program's by a relative error of at most 0.000076.
Values sent between devices are 32-bit elements; how exact they have to be, the bound alone decides.
A program may use at most 64 MiB of HBM per device.

v0:
```python
import jax
import jax.numpy as jnp
from jax import lax
from jax.sharding import PartitionSpec as P

PANEL = 512


def picked(x, axis, root):
    return lax.dynamic_index_in_dim(lax.all_gather(x, axis), root, 0, keepdims=False)


def cut_along(x, dim, size):
    before, after = (x.shape[:dim], x.shape[dim + 1 :])
    return jnp.moveaxis(x.reshape(*before, size, -1, *after), dim, 0)


def sent_and_summed(x, axis, dim):
    pieces = cut_along(x, dim, lax.axis_size(axis))
    arrived = lax.all_to_all(pieces, axis, split_axis=0, concat_axis=0, tiled=True)
    return arrived.sum(axis=0)


def product(left, right):
    return lax.dot_general(
        left,
        right,
        (((0,), (0,)), ((), ())),
        precision=lax.Precision.HIGHEST,
        preferred_element_type=jnp.float32,
    )


def gram_rows(left, panel_cols):
    return product(left, panel_cols)


def add_shift(values, shift_part, first_row, start):
    row_ids = first_row + jnp.arange(values.shape[0], dtype=jnp.int32)
    col_ids = jnp.arange(values.shape[1], dtype=jnp.int32)
    on_diag = row_ids[:, None] == start + col_ids[None, :]
    return values + jnp.where(on_diag, shift_part[:, None], jnp.zeros_like(values))


def on_device(constraint_rows, shift, group_rows, panel_index):
    width = constraint_rows.shape[1]
    groups = lax.axis_size("grp")
    col_idx = lax.axis_index("col")
    grp_idx = lax.axis_index("grp")
    share = width // groups
    start = panel_index[0] * PANEL
    owner = start // width
    local = start - owner * width
    live_count = lax.dynamic_index_in_dim(group_rows, grp_idx, keepdims=False)
    row_ids = jnp.arange(constraint_rows.shape[0], dtype=jnp.int32)
    masked = jnp.where(
        (row_ids < live_count)[:, None], constraint_rows, jnp.zeros_like(constraint_rows)
    )
    own_cols = lax.dynamic_slice_in_dim(masked, local, PANEL, 1)
    panel_cols = picked(own_cols, "col", owner)
    mine = sent_and_summed(gram_rows(masked, panel_cols), "grp", 0)
    shift_part = lax.dynamic_slice_in_dim(shift, grp_idx * share, share, 0)
    mine = add_shift(mine, shift_part, col_idx * width + grp_idx * share, start)
    from_owner = picked(mine, "col", owner)
    owner_shard = lax.all_gather(from_owner, "grp", axis=0, tiled=True)
    block = lax.dynamic_slice_in_dim(owner_shard, local, PANEL, 0)
    factor = jnp.linalg.cholesky(block)
    return lax.linalg.triangular_solve(factor, mine, left_side=False, lower=True, transpose_a=True)


def solution(mesh):
    placed = (P("grp", "col"), P("col"), P(), P())
    return jax.shard_map(
        on_device, mesh=mesh, in_specs=placed, out_specs=P(("col", "grp"), None), check_vma=False
    )
```

profile of v0, /device:TPU:1, one launch (start us, length us, event | category | flops | bytes accessed | tf_op | source)
XLA Modules:
  0.0 386.7 jit_solution(9339683539107075784)
XLA Ops:
  9.1 1.9 broadcast_select_fusion
  12.0 1.5 fusion.41
  13.5 1.9 copy.12
  15.5 70.8 %all-gather.8.cloned.1.call-done = f32[2048,512]{1,0:T(8,128)} async-done(((f32[256,512]{1,0:T(8,128)}), f32[2048,512]{1,0:T(8,128)}) %all-gather.8.cloned.1.call-update) | async-done | bytes 4194320 | tf_op jit(solution)/shard_map/all_gather | solution.py:10
  86.2 6.0 %fusion.1 = f32[16,128,512]{2,1,0:T(8,128)} fusion(f32[16,128,256]{2,1,0:T(8,128)S(1)} %bitcast.65, f32[8,256,512]{2,1,0:T(8,128)} %bitcast.66, s32[]{:T(128)S(6)} %select_n.47), kind=kOutput, calls=%fused_computation.15 | convolution fusion | flops 3221225472 | bytes 6815748 | tf_op jit(solution)/shard_map/dot_general | solution.py:25
  92.3 5.5 %all-to-all-start = ((f32[16,128,512]{2,1,0:T(8,128)}), f32[16,128,512]{2,1,0:T(8,128)}, u32[]{:S(2)}, u32[]{:S(2)}) async-start(f32[16,128,512]{2,1,0:T(8,128)} %fusion.1), calls=%async_computation | async-start | bytes 8388608 | tf_op jit(solution)/shard_map/all_to_all | solution.py:20
  98.6 48.9 %all-to-all-done = f32[16,128,512]{2,1,0:T(8,128)} async-done(((f32[16,128,512]{2,1,0:T(8,128)}), f32[16,128,512]{2,1,0:T(8,128)}, u32[]{:S(2)}, u32[]{:S(2)}) %all-to-all-start) | async-done | bytes 4194336 | tf_op jit(solution)/shard_map/all_to_all | solution.py:20
  147.5 2.6 reduce_sum.11
  151.2 50.8 %all-gather.6.cloned.1.call-done = f32[8,128,512]{2,1,0:T(8,128)} async-done(((f32[1,128,512]{2,1,0:T(8,128)}), f32[8,128,512]{2,1,0:T(8,128)}) %all-gather.6.cloned.1.call-update) | async-done | bytes 2097168 | tf_op jit(solution)/shard_map/all_gather | solution.py:10
  201.9 1.7 constant_dynamic-slice_fusion.2
  203.7 36.2 %all-gather.10.cloned.1.call-done = f32[1,2048,512]{2,1,0:T(8,128)} async-done(((f32[1,128,512]{2,1,0:T(8,128)}), f32[1,2048,512]{2,1,0:T(8,128)}) %all-gather.10.cloned.1.call-update) | async-done | bytes 4194320 | tf_op jit(solution)/shard_map/all_gather | solution.py:65
  243.0 11.7 %cholesky.104 = f32[128,128]{1,0:T(8,128)S(1)} custom-call(f32[128,128]{1,0:T(8,128)S(1)} %cholesky.266), custom_call_target="Cholesky" | custom-call | tf_op jit(solution)/shard_map/jit(cholesky)/cholesky | solution.py:67
  254.9 9.8 %custom-call.30 = f32[1,128,128]{1,2,0:T(8,128)S(1)} custom-call(f32[1,128,128]{2,1,0:T(8,128)S(1)} %get-tuple-element.32), custom_call_target="InvertDiagBlocksLowerTriangular" | custom-call | tf_op jit(solution)/shard_map/jit(cholesky)/cholesky | solution.py:67
  265.4 11.7 %cholesky.217 = f32[128,128]{1,0:T(8,128)S(1)} custom-call(f32[128,128]{1,0:T(8,128)S(1)} %cholesky.270), custom_call_target="Cholesky" | custom-call | tf_op jit(solution)/shard_map/jit(cholesky)/cholesky | solution.py:67
  277.1 10.0 %custom-call.31 = f32[1,128,128]{1,2,0:T(8,128)S(1)} custom-call(f32[1,128,128]{2,1,0:T(8,128)S(1)} %get-tuple-element.29), custom_call_target="InvertDiagBlocksLowerTriangular" | custom-call | tf_op jit(solution)/shard_map/jit(cholesky)/cholesky | solution.py:67
  287.8 11.7 %cholesky.238 = f32[128,128]{1,0:T(8,128)S(1)} custom-call(f32[128,128]{1,0:T(8,128)S(1)} %cholesky.275), custom_call_target="Cholesky" | custom-call | tf_op jit(solution)/shard_map/jit(cholesky)/cholesky | solution.py:67
  300.2 9.8 %custom-call.32 = f32[1,128,128]{1,2,0:T(8,128)S(1)} custom-call(f32[1,128,128]{2,1,0:T(8,128)S(1)} %get-tuple-element.26), custom_call_target="InvertDiagBlocksLowerTriangular" | custom-call | tf_op jit(solution)/shard_map/jit(cholesky)/cholesky | solution.py:67
  310.6 11.7 %cholesky.255 = f32[128,128]{1,0:T(8,128)S(1)} custom-call(f32[128,128]{1,0:T(8,128)S(1)} %convolution_subtract_fusion.5), custom_call_target="Cholesky" | custom-call | tf_op jit(solution)/shard_map/jit(cholesky)/cholesky | solution.py:67
  326.6 10.1 %while.1 = (s32[]{:T(128)}, f32[512,512]{1,0:T(8,128)S(1)}, s32[4,2]{0,1:T(2,128)S(1)}, f32[4,128,128]{2,1,0:T(8,128)}, s32[]{:T(128)}) while((s32[]{:T(128)}, f32[512,512]{1,0:T(8,128)S(1)}, s32[4,2]{0,1:T(2,128)S(1)}, f32[4,128,128]{2,1,0:T(8,128)}, s32[]{:T(128)}) %tuple.27), condition=%wide.while_cond, body=%wide.while_body.sunk | while | flops 2 | bytes 132705 | solution.py:68
  327.2 1.9 bitcast_dynamic-update-slice_fusion.2
  329.8 1.9 bitcast_dynamic-update-slice_fusion.2
  332.3 1.9 bitcast_dynamic-update-slice_fusion.2
  334.8 1.9 bitcast_dynamic-update-slice_fusion.2
  336.8 40.1 %custom-call.33 = f32[4,128,128]{1,2,0:T(8,128)S(1)} custom-call(f32[4,128,128]{2,1,0:T(8,128)} %get-tuple-element.12), custom_call_target="InvertDiagBlocksLowerTriangular" | custom-call | tf_op jit(solution)/shard_map/triangular_solve | solution.py:68
  (57 shorter events, 17.9 us)
Async XLA Ops:
  6.5 79.7 %all-gather.8.cloned.1.call-start = ((), (), s32[]{:S(2)}) async-start(), calls=%async_computation.2 | async-start | bytes 4718592 | tf_op jit(solution)/shard_map/all_gather | solution.py:10
  9.1 2.9 copy-start
  92.3 55.2 %all-to-all-start = ((f32[16,128,512]{2,1,0:T(8,128)}), f32[16,128,512]{2,1,0:T(8,128)}, u32[]{:S(2)}, u32[]{:S(2)}) async-start(f32[16,128,512]{2,1,0:T(8,128)} %fusion.1), calls=%async_computation | async-start | bytes 8388608 | tf_op jit(solution)/shard_map/all_to_all | solution.py:20
  97.8 104.1 %all-gather.6.cloned.1.call-start = ((), (), s32[]{:S(2)}) async-start(), calls=%async_computation.1 | async-start | bytes 2359296 | tf_op jit(solution)/shard_map/all_gather | solution.py:10
  150.9 89.0 %all-gather.10.cloned.1.call-start = ((), (), s32[]{:S(2)}) async-start(), calls=%async_computation.3 | async-start | bytes 4456448 | tf_op jit(solution)/shard_map/all_gather | solution.py:65
Sparse Core Ops, SparseCore 0:
  12.1 74.0 all-gather.7
  151.1 50.8 all-gather.5
  203.7 36.1 all-gather.9
where the time goes:
time: 387 us
  waiting for transfers between devices  207 us (53%)
  other arithmetic  128 us (33%)
  local copies, waits for them, and re-layouts  19.2 us (5%)
  between operations  16.6 us (4%)
  matrix products  10.2 us (3%)
  starting transfers between devices  5.78 us (1%)
    all_gather x2, waiting for transfers between devices, picked(): lax.all_gather(x, axis)  122 us
    another operation x14, other arithmetic, on_device(): factor = jnp.linalg.cholesky(block)  78.8 us
    all_to_all x1, waiting for transfers between devices, sent_and_summed(): lax.all_to_all(pieces, axis, split_axis=0, concat_axis=0, tiled=True)  48.9 us
    another operation x4, other arithmetic, on_device(): lax.linalg.triangular_solve(factor, mine, left_side=False, lower=True, tr...  40.3 us
    all_gather x1, waiting for transfers between devices, on_device(): owner_shard = lax.all_gather(from_owner, 'grp', axis=0, tiled=True)  36.2 us
    another operation x12, local copies, waits for them, and re-layouts  10.1 us
  transfers between devices with their start and end apart: 4, of which 4 were waited for; matrix products, arithmetic and copies ran while one was open for 1% of the time, Pallas kernels for 0%

commit v1 on v0

--- a/solution.py
+++ b/solution.py
@@ -62,7 +62,9 @@
     shift_part = lax.dynamic_slice_in_dim(shift, grp_idx * share, share, 0)
     mine = add_shift(mine, shift_part, col_idx * width + grp_idx * share, start)
     from_owner = picked(mine, "col", owner)
-    owner_shard = lax.all_gather(from_owner, "grp", axis=0, tiled=True)
+    owner_shard = jnp.concatenate(
+        lax.all_to_all(jnp.stack([from_owner] * lax.axis_size("grp")), "grp", 0, 0), axis=0
+    )
     block = lax.dynamic_slice_in_dim(owner_shard, local, PANEL, 0)
     factor = jnp.linalg.cholesky(block)
     return lax.linalg.triangular_solve(factor, mine, left_side=False, lower=True, transpose_a=True)

time: 387 us -> 412 us (1.065)
  waiting for transfers between devices: 207 us -> 220 us
  local copies, waits for them, and re-layouts: 19.2 us -> 24.9 us
  starting transfers between devices: 5.78 us -> 11.1 us
    all_to_all x0 -> x1, waiting for transfers between devices: none -> 49.6 us  [on_device(): lax.all_to_all(jnp.stack([from_owner] * lax.axis_size('grp')), 'grp', 0, 0)]
    all_gather x1 -> x0, waiting for transfers between devices: 36.2 us -> none  [on_device(): owner_shard = lax.all_gather(from_owner, 'grp', axis=0, tiled=True)]
    all_to_all x0 -> x1, starting transfers between devices: none -> 5.53 us  [on_device(): lax.all_to_all(jnp.stack([from_owner] * lax.axis_size('grp')), 'grp', 0, 0)]
    another operation x12 -> x13, local copies, waits for them, and re-layouts: 10.1 us -> 13 us
where the time goes in v1:
time: 412 us
  waiting for transfers between devices  220 us (53%)
  other arithmetic  128 us (31%)
  local copies, waits for them, and re-layouts  24.9 us (6%)
  between operations  16.9 us (4%)
  starting transfers between devices  11.1 us (3%)
  matrix products  10.2 us (2%)
    all_gather x2, waiting for transfers between devices, picked(): lax.all_gather(x, axis)  122 us
    another operation x14, other arithmetic, on_device(): factor = jnp.linalg.cholesky(block)  78.8 us
    all_to_all x1, waiting for transfers between devices, on_device(): lax.all_to_all(jnp.stack([from_owner] * lax.axis_size('grp')), 'grp', 0, 0)  49.6 us
    all_to_all x1, waiting for transfers between devices, sent_and_summed(): lax.all_to_all(pieces, axis, split_axis=0, concat_axis=0, tiled=True)  48.9 us
    another operation x4, other arithmetic, on_device(): lax.linalg.triangular_solve(factor, mine, left_side=False, lower=True, tr...  40.3 us
    another operation x12, local copies, waits for them, and re-layouts  10.6 us
  transfers between devices with their start and end apart: 4, of which 4 were waited for; matrix products, arithmetic and copies ran while one was open for 1% of the time, Pallas kernels for 0%

profile of v1, /device:TPU:1, one launch (start us, length us, event | category | flops | bytes accessed | tf_op | source)
XLA Modules:
  0.0 411.6 jit_solution(11087863877796480209)
XLA Ops:
  9.1 1.9 broadcast_select_fusion
  15.5 70.8 %all-gather.6.cloned.1.call-done = f32[2048,512]{1,0:T(8,128)} async-done(((f32[256,512]{1,0:T(8,128)}), f32[2048,512]{1,0:T(8,128)}) %all-gather.6.cloned.1.call-update) | async-done | bytes 4194320 | tf_op jit(solution)/shard_map/all_gather | solution.py:10
  86.2 6.0 %fusion.1 = f32[16,128,512]{2,1,0:T(8,128)} fusion(f32[16,128,256]{2,1,0:T(8,128)S(1)} %bitcast.68, f32[8,256,512]{2,1,0:T(8,128)} %bitcast.69, s32[]{:T(128)S(6)} %select_n.47), kind=kOutput, calls=%fused_computation.16 | convolution fusion | flops 3221225472 | bytes 6815748 | tf_op jit(solution)/shard_map/dot_general | solution.py:25
  92.3 5.5 %all-to-all-start = ((f32[16,128,512]{2,1,0:T(8,128)}), f32[16,128,512]{2,1,0:T(8,128)}, u32[]{:S(2)}, u32[]{:S(2)}) async-start(f32[16,128,512]{2,1,0:T(8,128)} %fusion.1), calls=%async_computation | async-start | bytes 8388608 | tf_op jit(solution)/shard_map/all_to_all | solution.py:20
  98.6 48.9 %all-to-all-done = f32[16,128,512]{2,1,0:T(8,128)} async-done(((f32[16,128,512]{2,1,0:T(8,128)}), f32[16,128,512]{2,1,0:T(8,128)}, u32[]{:S(2)}, u32[]{:S(2)}) %all-to-all-start) | async-done | bytes 4194336 | tf_op jit(solution)/shard_map/all_to_all | solution.py:20
  147.5 2.6 reduce_sum.11
  150.9 51.0 %all-gather.4.cloned.1.call-done = f32[8,128,512]{2,1,0:T(8,128)} async-done(((f32[1,128,512]{2,1,0:T(8,128)}), f32[8,128,512]{2,1,0:T(8,128)}) %all-gather.4.cloned.1.call-update) | async-done | bytes 2097168 | tf_op jit(solution)/shard_map/all_gather | solution.py:10
  203.0 2.4 stack.2
  205.4 5.5 %all-to-all-start.1 = ((f32[16,128,512]{1,2,0:T(8,128)}), f32[16,128,512]{1,2,0:T(8,128)}, u32[]{:S(2)}, u32[]{:S(2)}) async-start(f32[16,128,512]{1,2,0:T(8,128)} %stack.2), calls=%async_computation.1 | async-start | bytes 8388608 | tf_op jit(solution)/shard_map/all_to_all | solution.py:66
  211.1 49.6 %all-to-all-done.1 = f32[16,128,512]{1,2,0:T(8,128)} async-done(((f32[16,128,512]{1,2,0:T(8,128)}), f32[16,128,512]{1,2,0:T(8,128)}, u32[]{:S(2)}, u32[]{:S(2)}) %all-to-all-start.1) | async-done | bytes 4194336 | tf_op jit(solution)/shard_map/all_to_all | solution.py:66
  260.6 2.7 copy_bitcast_fusion
  267.2 11.7 %cholesky.104 = f32[128,128]{1,0:T(8,128)S(1)} custom-call(f32[128,128]{1,0:T(8,128)S(1)} %cholesky.266), custom_call_target="Cholesky" | custom-call | tf_op jit(solution)/shard_map/jit(cholesky)/cholesky | solution.py:69
  279.1 9.8 %custom-call.30 = f32[1,128,128]{1,2,0:T(8,128)S(1)} custom-call(f32[1,128,128]{2,1,0:T(8,128)S(1)} %get-tuple-element.32), custom_call_target="InvertDiagBlocksLowerTriangular" | custom-call | tf_op jit(solution)/shard_map/jit(cholesky)/cholesky | solution.py:69
  289.6 11.7 %cholesky.217 = f32[128,128]{1,0:T(8,128)S(1)} custom-call(f32[128,128]{1,0:T(8,128)S(1)} %cholesky.270), custom_call_target="Cholesky" | custom-call | tf_op jit(solution)/shard_map/jit(cholesky)/cholesky | solution.py:69
  301.3 10.0 %custom-call.31 = f32[1,128,128]{1,2,0:T(8,128)S(1)} custom-call(f32[1,128,128]{2,1,0:T(8,128)S(1)} %get-tuple-element.29), custom_call_target="InvertDiagBlocksLowerTriangular" | custom-call | tf_op jit(solution)/shard_map/jit(cholesky)/cholesky | solution.py:69
  312.0 11.7 %cholesky.238 = f32[128,128]{1,0:T(8,128)S(1)} custom-call(f32[128,128]{1,0:T(8,128)S(1)} %cholesky.275), custom_call_target="Cholesky" | custom-call | tf_op jit(solution)/shard_map/jit(cholesky)/cholesky | solution.py:69
  324.4 9.8 %custom-call.32 = f32[1,128,128]{1,2,0:T(8,128)S(1)} custom-call(f32[1,128,128]{2,1,0:T(8,128)S(1)} %get-tuple-element.26), custom_call_target="InvertDiagBlocksLowerTriangular" | custom-call | tf_op jit(solution)/shard_map/jit(cholesky)/cholesky | solution.py:69
  334.8 11.9 %cholesky.255 = f32[128,128]{1,0:T(8,128)S(1)} custom-call(f32[128,128]{1,0:T(8,128)S(1)} %convolution_subtract_fusion.5), custom_call_target="Cholesky" | custom-call | tf_op jit(solution)/shard_map/jit(cholesky)/cholesky | solution.py:69
  350.8 10.6 %while.1 = (s32[]{:T(128)}, f32[512,512]{1,0:T(8,128)S(1)}, s32[4,2]{0,1:T(2,128)S(1)}, f32[4,128,128]{2,1,0:T(8,128)}, s32[]{:T(128)}) while((s32[]{:T(128)}, f32[512,512]{1,0:T(8,128)S(1)}, s32[4,2]{0,1:T(2,128)S(1)}, f32[4,128,128]{2,1,0:T(8,128)}, s32[]{:T(128)}) %tuple.27), condition=%wide.while_cond, body=%wide.while_body.sunk | while | flops 2 | bytes 132705 | solution.py:70
  351.5 2.0 bitcast_dynamic-update-slice_fusion.2
  354.1 2.0 bitcast_dynamic-update-slice_fusion.2
  356.8 2.0 bitcast_dynamic-update-slice_fusion.2
  359.4 2.0 bitcast_dynamic-update-slice_fusion.2
  361.4 40.1 %custom-call.33 = f32[4,128,128]{1,2,0:T(8,128)S(1)} custom-call(f32[4,128,128]{2,1,0:T(8,128)} %get-tuple-element.12), custom_call_target="InvertDiagBlocksLowerTriangular" | custom-call | tf_op jit(solution)/shard_map/triangular_solve | solution.py:70
  (61 shorter events, 23.1 us)
Async XLA Ops:
  6.5 79.7 %all-gather.6.cloned.1.call-start = ((), (), s32[]{:S(2)}) async-start(), calls=%async_computation.3 | async-start | bytes 4718592 | tf_op jit(solution)/shard_map/all_gather | solution.py:10
  9.1 2.9 copy-start.1
  92.3 55.2 %all-to-all-start = ((f32[16,128,512]{2,1,0:T(8,128)}), f32[16,128,512]{2,1,0:T(8,128)}, u32[]{:S(2)}, u32[]{:S(2)}) async-start(f32[16,128,512]{2,1,0:T(8,128)} %fusion.1), calls=%async_computation | async-start | bytes 8388608 | tf_op jit(solution)/shard_map/all_to_all | solution.py:20
  97.8 104.1 %all-gather.4.cloned.1.call-start = ((), (), s32[]{:S(2)}) async-start(), calls=%async_computation.2 | async-start | bytes 2359296 | tf_op jit(solution)/shard_map/all_gather | solution.py:10
  205.4 55.2 %all-to-all-start.1 = ((f32[16,128,512]{1,2,0:T(8,128)}), f32[16,128,512]{1,2,0:T(8,128)}, u32[]{:S(2)}, u32[]{:S(2)}) async-start(f32[16,128,512]{1,2,0:T(8,128)} %stack.2), calls=%async_computation.1 | async-start | bytes 8388608 | tf_op jit(solution)/shard_map/all_to_all | solution.py:66
  263.3 1.9 copy-start
Sparse Core Ops, SparseCore 0:
  12.1 74.0 all-gather.5
  151.1 50.8 all-gather.3
